TPU v7x, 32 devices: a whole 2x2x4 slice. The times are simulated.
32 devices in a mesh: gx: 8 (over z, y), gy: 4 (over x, core).
Axes of the slice: x: 2, y: 2, z: 4, core: 2. Of those that a mesh axis runs over, the one named last changes fastest.
Arguments:
- tracer: float32 [1, 24, 128, 512], P(None, None, 'gx', 'gy'), may hold values from -3 to 3
- kappa: float32 [128, 512], P('gx', 'gy'), may hold values from 0.06 to 0.24
- dkappa: float32 [128, 512], P('gx', 'gy'), may hold values from -6 to 6
- precision_weight: float32 [24, 24], replicated, may hold values from -0.08 to 2.08, as said below
- observed: int32 [4, 8, 32], P(None, 'gx', 'gy'), may hold values 0 or 1
Outputs:
- hess_vec: float32 [128, 512], P('gx', 'gy')
- gram: float32 [24, 24], replicated
- curvature: float32 [], replicated
Inputs may be any that keep to these rules, and one draw needn't show every extreme that they name: `precision_weight`: symmetric; each diagonal entry exceeds the sum of the magnitudes of the other entries of its row.
All inputs are finite; a program needn't handle non-finite values. No bound on the sum of `observed` on one device may be relied on, other than what follows from the above.
Results may differ from a plain program's by a relative error of at most 0.0001.
Values sent between devices are 32-bit elements; how exact they have to be, the bound alone decides.
A program may use at most 64 MiB of HBM per device.

v0:
```python
import functools

import jax
import jax.numpy as jnp
from jax import lax
from jax.experimental import pallas as pl
from jax.experimental.pallas import tpu as pltpu
from jax.sharding import PartitionSpec as P

STEPS = 4
HALO = 2 * STEPS
LANES = 128
MESH = pl.DeviceIdType.MESH
BF = jnp.bfloat16
F32 = jnp.float32


def east(v):
    return pltpu.roll(v, LANES - 1, v.ndim - 1)


def west(v):
    return pltpu.roll(v, 1, v.ndim - 1)


def sweep(lo, hi, n, body):
    count = (hi - lo) // n
    if count > 1:

        def one(i, carry):
            body(lo + i * n, n)
            return carry

        lax.fori_loop(0, count, one, 0)
    elif count == 1:
        body(lo, n)
    rest = (hi - lo) - count * n
    if rest:
        body(lo + count * n, rest)


def split(x):
    high = x.astype(BF).astype(F32)
    return high, x - high


def kernel(
    nx,
    ny,
    tracer_ref,
    kappa_ref,
    dkappa_ref,
    weight_ref,
    observed_ref,
    hess_ref,
    gram_ref,
    curv_ref,
    mb,
    mt,
    ma,
    mp,
    mc,
    mm,
    mge,
    mgs,
    sb,
    st,
    sa,
    sp,
    sc,
    sm,
    sge,
    sgs,
    edges,
    rim,
    cbuf,
    sums_y,
    sums_x,
    send_sem,
    recv_sem,
    ysend,
    yrecv,
    xsend,
    xrecv,
):
    gx = lax.axis_index("gx")
    gy = lax.axis_index("gy")
    north, south = lax.rem(gx + nx - 1, nx), lax.rem(gx + 1, nx)
    left, right = lax.rem(gy + ny - 1, ny), lax.rem(gy + 1, ny)

    barrier = pltpu.get_barrier_semaphore()
    friends = [(gx, lax.rem(gy + i, ny)) for i in range(1, ny)]
    friends += [(lax.rem(gx + i, nx), gy) for i in range(1, nx)]
    friends += [(north, left), (north, right), (south, left), (south, right)]
    for friend in friends:
        pl.semaphore_signal(barrier, inc=1, device_id=friend, device_id_type=MESH)

    lane = lax.broadcasted_iota(jnp.int32, (8, LANES), 1)
    own = jnp.swapaxes(tracer_ref[0], 0, 1)
    mb[0, 8:24] = own.reshape(16, 3, 8, LANES)
    cbuf[1, 3] = kappa_ref[0:8]
    cbuf[1, 4] = dkappa_ref[0:8]
    cbuf[1, 6] = kappa_ref[8:16]
    cbuf[1, 7] = dkappa_ref[8:16]
    tiles = observed_ref.shape[2]
    seen = observed_ref[:, 0, :].astype(F32)
    mask = jnp.zeros((STEPS, LANES), F32)
    spot = lax.broadcasted_iota(jnp.int32, (STEPS, LANES), 1) // (LANES // tiles)
    for i in range(tiles):
        mask = jnp.where(spot == i, seen[:, i : i + 1], mask)
    cbuf[1, 5] = jnp.concatenate([mask, jnp.zeros((8 - STEPS, LANES), F32)], axis=0)
    for half in range(2):
        packed = jnp.zeros((3, 8, LANES), F32)
        for s in range(8):
            row = mb[0, 8 + 8 * half + s]
            both = jnp.where(lane < 8, row, pltpu.roll(row, 16, 2))
            if s:
                both = pltpu.roll(both, 16 * s, 2)
            packed = jnp.where(lane // 16 == s, both, packed)
        edges[half] = packed

    pl.semaphore_wait(barrier, len(friends))

    plan = [
        (mb.at[0, 8:16], mb.at[0, 24:32], (north, gy)),
        (mb.at[0, 16:24], mb.at[0, 0:8], (south, gy)),
        (edges, rim.at[0, 1:3], (gx, right)),
        (edges, rim.at[1, 1:3], (gx, left)),
        (edges.at[0:1], rim.at[0, 3:4], (north, right)),
        (edges.at[0:1], rim.at[1, 3:4], (north, left)),
        (edges.at[1:2], rim.at[0, 0:1], (south, right)),
        (edges.at[1:2], rim.at[1, 0:1], (south, left)),
    ]
    mine = cbuf.at[1]
    plan += [
        (mine.at[3:6], cbuf.at[1, 8:11], (north, gy)),
        (mine.at[5:8], cbuf.at[1, 0:3], (south, gy)),
        (mine.at[3:8], cbuf.at[0, 3:8], (gx, right)),
        (mine.at[3:8], cbuf.at[2, 3:8], (gx, left)),
        (mine.at[3:6], cbuf.at[0, 8:11], (north, right)),
        (mine.at[3:6], cbuf.at[2, 8:11], (north, left)),
        (mine.at[5:8], cbuf.at[0, 0:3], (south, right)),
        (mine.at[5:8], cbuf.at[2, 0:3], (south, left)),
    ]
    copies = []
    for i, (src, dst, where) in enumerate(plan):
        copy = pltpu.make_async_remote_copy(
            src_ref=src,
            dst_ref=dst,
            send_sem=send_sem.at[i],
            recv_sem=recv_sem.at[i],
            device_id=where,
            device_id_type=MESH,
        )
        copy.start()
        copies.append(copy)

    weight_high, weight_low = split(weight_ref[...])
    weight_rows = jnp.concatenate([weight_high, weight_low], axis=0)
    weights = jnp.concatenate([weight_rows, weight_rows], axis=1).astype(BF)

    for copy in copies[8:]:
        copy.wait_recv()

    ok_left = jnp.where(gy > 0, 1.0, 0.0).astype(F32)
    ok_right = jnp.where(gy < ny - 1, 1.0, 0.0).astype(F32)
    one = jnp.ones((8, LANES), F32)
    inside_rim = jnp.where(lane % 16 < 8, ok_right * one, ok_left * one)
    domain_a = jnp.where(lane >= 112, inside_rim, one)
    domain = domain_a * pltpu.roll(domain_a, 64, 1)

    def sides(mid, rim_part):
        ax = mid.ndim - 1
        return jnp.where(
            lane < 16,
            mid,
            jnp.where(
                lane >= 112,
                rim_part,
                jnp.where(lane >= 96, pltpu.roll(mid, 112, ax), 0.0),
            ),
        )

    cmid = cbuf[1]
    crim = jnp.where(lane >= 120, cbuf[0], pltpu.roll(cbuf[2], 112, 2)) * inside_rim
    cside = sides(cmid, crim)

    def coefficients(kap, dk, out):
        rows = kap.shape[0]
        for index, field in ((0, kap), (2, dk)):
            face = 0.5 * (field + east(field))
            for r in range(1, rows - 1):
                out[index, r] = jnp.broadcast_to(face[r : r + 1], (8, LANES))
            face = 0.5 * (field[: rows - 1] + field[1:])
            for r in range(rows - 1):
                out[index + 1, r] = jnp.broadcast_to(face[r : r + 1], (8, LANES))

    def stack(source, picks):
        return jnp.concatenate([source[i] for i in picks], axis=0)

    k_main = stack(cmid, (1, 3, 6, 8))
    d_main = stack(cmid, (2, 4, 7, 9))
    k_all = stack(cside, (1, 3, 6, 8))
    d_all = stack(cside, (2, 4, 7, 9))
    k_side = k_all[:24] + pltpu.roll(k_all[8:], 64, 1)
    d_side = d_all[:24] + pltpu.roll(d_all[8:], 64, 1)
    coefficients(k_main, d_main, mc)
    coefficients(k_side, d_side, sc)

    side_mask = [
        cside[0] + pltpu.roll(cside[5], 64, 1),
        cside[5] + pltpu.roll(cside[5], 64, 1),
        cside[5] + pltpu.roll(cside[10], 64, 1),
    ]
    main_mask = [cmid[0], cmid[5], cmid[10]]
    for k in range(STEPS):
        for masks, out, cuts in (
            (main_mask, mm, (4, 8, 24, 28)),
            (side_mask, sm, (4, 8, 16, 20)),
        ):
            for part in range(3):
                wide = jnp.broadcast_to(masks[part][k : k + 1], (8, LANES))
                for r in range(cuts[part], cuts[part + 1]):
                    out[k, r] = wide

    def laplace(field, lo, hi):
        mid = field[lo:hi]
        return 4.0 * mid - east(mid) - west(mid) - field[lo - 1 : hi - 1] - field[lo + 1 : hi + 1]

    wide_lane = lax.broadcasted_iota(jnp.int32, (16, LANES), 1)

    def assemble(main, side):
        both = jnp.concatenate([side, pltpu.roll(side, 64, 1)], axis=0)
        return jnp.where(
            wide_lane < 8,
            both,
            jnp.where(wide_lane >= 120, pltpu.roll(both, 16, 1), main),
        )

    reg = assemble(laplace(d_main, 8, 24), laplace(d_side, 8, 16))
    energy = dkappa_ref[...] * reg
    energy = energy[0:8] + energy[8:16]

    for copy in copies[:8]:
        copy.wait_recv()

    for g in range(4):
        held = jnp.where(lane % 16 < 8, rim[1, g], rim[0, g]) * inside_rim
        for s in range(8):
            e = 8 * g + s
            turn = (112 - 16 * s) % LANES
            part = held if turn == 0 else pltpu.roll(held, turn, 2)
            cell = sides(mb[0, e], part)
            if e < 24:
                sb[0, e] = cell
            if e >= 8:
                sb[0, e - 8] = sb[0, e - 8] + pltpu.roll(cell, 64, 2)

    def forward(rows, base, tan, coef, dom, k):
        def body(r, n):
            b = base[k, pl.ds(r - 1, n + 2)]
            mid = b[1:-1]
            down = b[1:] - b[:-1]
            across = east(mid) - mid
            ke = coef[0, pl.ds(r, n)][:, None]
            ks = coef[1, pl.ds(r - 1, n + 1)][:, None]
            de = coef[2, pl.ds(r, n)][:, None]
            ds = coef[3, pl.ds(r - 1, n + 1)][:, None]

            def close(fs, fe):
                total = (fs[1:] - fs[:-1]) + (fe - west(fe))
                return total if dom is None else total * dom

            if k < STEPS - 1:
                base[k + 1, pl.ds(r, n)] = mid + close(ks * down, ke * across)
            fs = ds * down
            fe = de * across
            if k == 0:
                tan[0, pl.ds(r, n)] = close(fs, fe)
            else:
                t = tan[k - 1, pl.ds(r - 1, n + 2)]
                tmid = t[1:-1]
                fs = fs + ks * (t[1:] - t[:-1])
                fe = fe + ke * (east(tmid) - tmid)
                tan[k, pl.ds(r, n)] = tmid + close(fs, fe)

        sweep(k + 1, rows - k - 1, 4, body)

    for k in range(STEPS):
        forward(32, mb, mt, mc, None, k)
        forward(24, sb, st, sc, domain, k)

    main_cells = jnp.where((lane >= 8) & (lane < 120), 1.0, 0.0).astype(F32)
    side_cells = jnp.where(
        (lane < 8) | ((lane >= 104) & (lane < 112)) | ((lane >= 64) & (lane < 72)) | ((lane >= 40) & (lane < 48)),
        1.0,
        0.0,
    ).astype(F32)
    total = jnp.zeros((48, 48), F32)
    for tan, msk, cells, rows in ((mt, mm, main_cells, 16), (st, sm, side_cells, 8)):

        def gather(i, acc, tan=tan, msk=msk, cells=cells):
            r = 8 + 2 * i
            for k in range(STEPS):
                field = tan[k, pl.ds(r, 2)] * (msk[k, pl.ds(r, 2)] * cells)[:, None]
                high, low = split(field.reshape(2, 24, LANES))
                both = jnp.concatenate([high, low], axis=1)
                both = jnp.concatenate([both[0], both[1]], axis=1).astype(BF)
                acc = acc + lax.dot_general(
                    both, both, (((1,), (1,)), ((), ())), preferred_element_type=F32
                )
            return acc

        total = lax.fori_loop(0, rows // 2, gather, total)
    gram = total[:24, :24] + (total[:24, 24:] + total[24:, :24]) + total[24:, 24:]
    gram = jnp.concatenate([gram, jnp.zeros((24, LANES - 24), F32)], axis=1)

    sums_y[gy, 0:3] = gram.reshape(3, 8, LANES)
    sums_y[gy, 3] = energy
    ycopies = []
    for i in range(1, ny):
        copy = pltpu.make_async_remote_copy(
            src_ref=sums_y.at[gy],
            dst_ref=sums_y.at[gy],
            send_sem=ysend.at[i],
            recv_sem=yrecv.at[i],
            device_id=(gx, lax.rem(gy + i, ny)),
            device_id_type=MESH,
        )
        copy.start()
        ycopies.append(copy)

    def weigh(rows, base, out):
        def body(r, n):
            for k in range(STEPS):
                field = base[k, pl.ds(r, n)].reshape(n, 24, LANES)
                high, low = split(field)
                both = jnp.concatenate([high, low], axis=1)
                both = jnp.concatenate([both[i] for i in range(n)], axis=1).astype(BF)
                got = jnp.dot(weights, both, preferred_element_type=F32)
                got = got[:24] + got[24:]
                for i in range(n):
                    out[k, r + i] = got[:, i * LANES : (i + 1) * LANES].reshape(3, 8, LANES)

        sweep(7, rows - 7, 2, body)

    weigh(32, mb, mp)
    weigh(24, sb, sp)

    def backward(rows, tan, adj, coef, msk, dom, k):
        def last(r, n):
            adj[3, pl.ds(r, n)] = tan[3, pl.ds(r, n)] * msk[3, pl.ds(r, n)][:, None]

        def body(r, n):
            a = adj[k, pl.ds(r - 1, n + 2)]
            mid = a[1:-1]
            ke = coef[0, pl.ds(r, n)][:, None]
            ks = coef[1, pl.ds(r - 1, n + 1)][:, None]
            fs = ks * (a[1:] - a[:-1])
            fe = ke * (east(mid) - mid)
            change = (fs[1:] - fs[:-1]) + (fe - west(fe))
            if dom is not None:
                change = change * dom
            source = tan[k - 1, pl.ds(r, n)] * msk[k - 1, pl.ds(r, n)][:, None]
            adj[k - 1, pl.ds(r, n)] = mid + change + source

        if k == STEPS:
            sweep(4, rows - 4, 4, last)
        else:
            sweep(8 - k, rows - 8 + k, 4, body)

    for k in range(STEPS, 1, -1):
        backward(32, mt, ma, mc, mm, None, k)
        backward(24, st, sa, sc, sm, domain, k)

    for copy in ycopies:
        copy.wait_recv()
    part = sums_y[0]
    for i in range(1, ny):
        part = part + sums_y[i]
    sums_x[gx] = part
    xcopies = []
    for i in range(1, nx):
        copy = pltpu.make_async_remote_copy(
            src_ref=sums_x.at[gx],
            dst_ref=sums_x.at[gx],
            send_sem=xsend.at[i],
            recv_sem=xrecv.at[i],
            device_id=(lax.rem(gx + i, nx), gy),
            device_id_type=MESH,
        )
        copy.start()
        xcopies.append(copy)

    backward(32, mt, ma, mc, mm, None, 1)
    backward(24, st, sa, sc, sm, domain, 1)

    def products(rows, weighed, adj, ge, gs):
        def body(r, n):
            acc_e = jnp.zeros((n, 8, LANES), F32)
            acc_s = jnp.zeros((n, 8, LANES), F32)
            for k in range(STEPS):
                b = weighed[k, pl.ds(r, n + 1)]
                a = adj[k, pl.ds(r, n + 1)]
                acc_s = acc_s + jnp.sum((b[1:] - b[:-1]) * (a[1:] - a[:-1]), axis=1)
                b = b[:-1]
                a = a[:-1]
                acc_e = acc_e + jnp.sum((east(b) - b) * (east(a) - a), axis=1)
            ge[pl.ds(r, n)] = acc_e
            gs[pl.ds(r, n)] = acc_s

        sweep(7, rows - 8, 2, body)
        across = jnp.sum(ge[8 : rows - 8], axis=1)
        down = jnp.sum(gs[7 : rows - 8], axis=1)
        return -0.5 * (across + west(across) + down[1:] + down[:-1])

    main = products(32, mp, ma, mge, mgs)
    side = products(24, sp, sa, sge, sgs)
    hess_ref[...] = assemble(main, side) + 0.5 * reg

    for copy in xcopies:
        copy.wait_recv()
    part = sums_x[0]
    for i in range(1, nx):
        part = part + sums_x[i]
    scale = 1.0 / (16 * LANES * nx * ny)
    whole = part[0:3].reshape(24, LANES)[:, :24] * scale
    gram_ref[...] = whole
    quad = jnp.sum(jnp.sum(weight_ref[...] * whole, axis=1, keepdims=True), axis=0, keepdims=True)
    energy = jnp.sum(jnp.sum(part[3], axis=1, keepdims=True), axis=0, keepdims=True)
    curv_ref[...] = quad + (0.5 * scale) * energy

    for copy in copies + ycopies + xcopies:
        copy.wait_send()


def body(tracer, kappa, dkappa, precision_weight, observed):
    nx, ny = lax.axis_size("gx"), lax.axis_size("gy")

    def region(rows):
        field = pltpu.VMEM((STEPS, rows, 3, 8, LANES), F32)
        row = pltpu.VMEM((rows, 8, LANES), F32)
        return [field] * 4 + [pltpu.VMEM((4, rows, 8, LANES), F32)] * 2 + [row] * 2

    vmem = pl.BlockSpec(memory_space=pltpu.VMEM)
    hess, gram, curv = pl.pallas_call(
        functools.partial(kernel, nx, ny),
        out_shape=(
            jax.ShapeDtypeStruct(kappa.shape, F32),
            jax.ShapeDtypeStruct(precision_weight.shape, F32),
            jax.ShapeDtypeStruct((1, 1), F32),
        ),
        in_specs=[vmem] * 5,
        out_specs=(vmem,) * 3,
        scratch_shapes=region(32)
        + region(24)
        + [
            pltpu.VMEM((2, 3, 8, LANES), F32),
            pltpu.VMEM((2, 4, 3, 8, LANES), F32),
            pltpu.VMEM((3, 11, 8, LANES), F32),
            pltpu.VMEM((ny, 4, 8, LANES), F32),
            pltpu.VMEM((nx, 4, 8, LANES), F32),
            pltpu.SemaphoreType.DMA((16,)),
            pltpu.SemaphoreType.DMA((16,)),
            pltpu.SemaphoreType.DMA((ny,)),
            pltpu.SemaphoreType.DMA((ny,)),
            pltpu.SemaphoreType.DMA((nx,)),
            pltpu.SemaphoreType.DMA((nx,)),
        ],
        compiler_params=pltpu.CompilerParams(
            collective_id=0, has_side_effects=True, vmem_limit_bytes=40 * 1024 * 1024
        ),
    )(tracer, kappa, dkappa, precision_weight, observed)
    return hess, gram, curv.reshape(())


def solution(mesh):
    placed = (P(None, None, "gx", "gy"), P("gx", "gy"), P("gx", "gy"), P(), P(None, "gx", "gy"))
    return jax.shard_map(
        body, mesh=mesh, in_specs=placed, out_specs=(P("gx", "gy"), P(), P()), check_vma=False
    )
```

profile of v0, /device:TPU:0, one launch (start us, length us, event | category | flops | bytes accessed | tf_op | source)
XLA Modules:
  0.0 43.9 jit_solution(9504723908972655429)
XLA Ops:
  0.6 0.0 copy-start
  0.6 0.9 %copy-done = f32[1,24,16,128]{3,2,1,0:T(8,128)S(1)} copy-done((f32[1,24,16,128]{3,2,1,0:T(8,128)S(1)}, f32[1,24,16,128]{3,2,1,0:T(8,128)}, u32[]{:S(2)}) %copy-start) | copy-done | bytes 196632
  1.6 0.0 copy-start.1
  1.6 0.7 %copy-done.1 = f32[24,24]{1,0:T(8,128)S(1)} copy-done((f32[24,24]{1,0:T(8,128)S(1)}, f32[24,24]{1,0:T(8,128)}, u32[]{:S(2)}) %copy-start.1) | copy-done | bytes 2328
  2.3 0.0 copy-start.2
  2.3 0.7 %copy-done.2 = f32[16,128]{1,0:T(8,128)S(1)} copy-done((f32[16,128]{1,0:T(8,128)S(1)}, f32[16,128]{1,0:T(8,128)}, u32[]{:S(2)}) %copy-start.2) | copy-done | bytes 8216
  3.0 0.0 copy-start.3
  3.0 0.7 %copy-done.3 = f32[16,128]{1,0:T(8,128)S(1)} copy-done((f32[16,128]{1,0:T(8,128)S(1)}, f32[16,128]{1,0:T(8,128)}, u32[]{:S(2)}) %copy-start.3) | copy-done | bytes 8216
  3.7 0.0 copy-start.4
  3.7 0.7 %copy-done.4 = s32[4,1,8]{2,1,0:T(1,128)S(1)} copy-done((s32[4,1,8]{2,1,0:T(1,128)S(1)}, s32[4,1,8]{2,1,0:T(1,128)}, u32[]{:S(2)}) %copy-start.4) | copy-done | bytes 152
  4.3 36.6 %shard_map.76 = (f32[16,128]{1,0:T(8,128)S(1)}, f32[24,24]{1,0:T(8,128)S(1)}, f32[1,1]{1,0:T(1,128)}) custom-call(f32[1,24,16,128]{3,2,1,0:T(8,128)S(1)} %copy-done, f32[16,128]{1,0:T(8,128)S(1)} %copy-done.2, f32[16,128]{1,0:T(8,128)S(1)} %copy-done.3, f32[24,24]{1,0:T(8,128)S(1)} %copy-done.1, s32[4,1,8]{2,1,0:T(1,128)S(1)} %copy-done.4), custom_call_target="tpu_custom_call" | custom-call | tf_op jit(solution)/shard_map/pallas_call | solution.py:446
  41.0 0.6 %copy.11 = f32[16,128]{1,0:T(8,128)} copy(f32[16,128]{1,0:T(8,128)S(1)} %get-tuple-element.12) | data formatting | bytes 16384
  41.6 0.6 %copy.12 = f32[24,24]{1,0:T(8,128)} copy(f32[24,24]{1,0:T(8,128)S(1)} %get-tuple-element.13) | data formatting | bytes 4608
Async XLA Ops:
  0.6 0.9 %copy-start = (f32[1,24,16,128]{3,2,1,0:T(8,128)S(1)}, f32[1,24,16,128]{3,2,1,0:T(8,128)}, u32[]{:S(2)}) copy-start(f32[1,24,16,128]{3,2,1,0:T(8,128)} %tracer_ref.1) | copy-start | bytes 589828
  1.6 0.7 %copy-start.1 = (f32[24,24]{1,0:T(8,128)S(1)}, f32[24,24]{1,0:T(8,128)}, u32[]{:S(2)}) copy-start(f32[24,24]{1,0:T(8,128)} %weight_ref.1) | copy-start | bytes 6916
  2.3 0.7 %copy-start.2 = (f32[16,128]{1,0:T(8,128)S(1)}, f32[16,128]{1,0:T(8,128)}, u32[]{:S(2)}) copy-start(f32[16,128]{1,0:T(8,128)} %kappa_ref.1) | copy-start | bytes 24580
  3.0 0.7 %copy-start.3 = (f32[16,128]{1,0:T(8,128)S(1)}, f32[16,128]{1,0:T(8,128)}, u32[]{:S(2)}) copy-start(f32[16,128]{1,0:T(8,128)} %dkappa_ref.1) | copy-start | bytes 24580
  3.7 0.7 %copy-start.4 = (s32[4,1,8]{2,1,0:T(1,128)S(1)}, s32[4,1,8]{2,1,0:T(1,128)}, u32[]{:S(2)}) copy-start(s32[4,1,8]{2,1,0:T(1,128)} %observed_ref.1) | copy-start | bytes 388
where the time goes:
time: 44.3 us; the launch traced here: 43.9 us
  Pallas kernels  36.6 us (83%)
  local copies, waits for them, and re-layouts  4.9 us (11%)
  between operations  2.34 us (5%)
    pallas_call x1, Pallas kernels, body(): pl.pallas_call(functools.partial(kernel, nx, ny), out_shape=(jax.ShapeDty...  36.6 us
    unnamed x12, local copies, waits for them, and re-layouts  4.9 us

commit v1 on v0

--- a/solution.py
+++ b/solution.py
@@ -24,19 +24,8 @@
 
 
 def sweep(lo, hi, n, body):
-    count = (hi - lo) // n
-    if count > 1:
-
-        def one(i, carry):
-            body(lo + i * n, n)
-            return carry
-
-        lax.fori_loop(0, count, one, 0)
-    elif count == 1:
-        body(lo, n)
-    rest = (hi - lo) - count * n
-    if rest:
-        body(lo + count * n, rest)
+    for r in range(lo, hi, n):
+        body(r, min(n, hi - r))
 
 
 def split(x):
@@ -311,7 +300,8 @@
                 )
             return acc
 
-        total = lax.fori_loop(0, rows // 2, gather, total)
+        for i in range(rows // 2):
+            total = gather(i, total)
     gram = total[:24, :24] + (total[:24, 24:] + total[24:, :24]) + total[24:, 24:]
     gram = jnp.concatenate([gram, jnp.zeros((24, LANES - 24), F32)], axis=1)
 

time: 44.3 us -> 37.4 us (0.84)
  Pallas kernels: 36.6 us -> 29.8 us
    pallas_call x1, Pallas kernels: 36.6 us -> 29.8 us  [body(): pl.pallas_call(functools.partial(kernel, nx, ny), out_shape=(jax.ShapeDty...]
where the time goes in v1:
time: 37.4 us; the launch traced here: 37 us
  Pallas kernels  29.8 us (80%)
  local copies, waits for them, and re-layouts  4.9 us (13%)
  between operations  2.34 us (6%)
    pallas_call x1, Pallas kernels, body(): pl.pallas_call(functools.partial(kernel, nx, ny), out_shape=(jax.ShapeDty...  29.8 us
    unnamed x12, local copies, waits for them, and re-layouts  4.9 us

profile of v1, /device:TPU:0, one launch (start us, length us, event | category | flops | bytes accessed | tf_op | source)
XLA Modules:
  0.0 37.0 jit_solution(8776803813187430977)
XLA Ops:
  0.6 0.0 copy-start
  0.6 0.9 %copy-done = f32[1,24,16,128]{3,2,1,0:T(8,128)S(1)} copy-done((f32[1,24,16,128]{3,2,1,0:T(8,128)S(1)}, f32[1,24,16,128]{3,2,1,0:T(8,128)}, u32[]{:S(2)}) %copy-start) | copy-done | bytes 196632
  1.6 0.0 copy-start.1
  1.6 0.7 %copy-done.1 = f32[24,24]{1,0:T(8,128)S(1)} copy-done((f32[24,24]{1,0:T(8,128)S(1)}, f32[24,24]{1,0:T(8,128)}, u32[]{:S(2)}) %copy-start.1) | copy-done | bytes 2328
  2.3 0.0 copy-start.2
  2.3 0.7 %copy-done.2 = f32[16,128]{1,0:T(8,128)S(1)} copy-done((f32[16,128]{1,0:T(8,128)S(1)}, f32[16,128]{1,0:T(8,128)}, u32[]{:S(2)}) %copy-start.2) | copy-done | bytes 8216
  3.0 0.0 copy-start.3
  3.0 0.7 %copy-done.3 = f32[16,128]{1,0:T(8,128)S(1)} copy-done((f32[16,128]{1,0:T(8,128)S(1)}, f32[16,128]{1,0:T(8,128)}, u32[]{:S(2)}) %copy-start.3) | copy-done | bytes 8216
  3.7 0.0 copy-start.4
  3.7 0.7 %copy-done.4 = s32[4,1,8]{2,1,0:T(1,128)S(1)} copy-done((s32[4,1,8]{2,1,0:T(1,128)S(1)}, s32[4,1,8]{2,1,0:T(1,128)}, u32[]{:S(2)}) %copy-start.4) | copy-done | bytes 152
  4.3 29.8 %shard_map.76 = (f32[16,128]{1,0:T(8,128)S(1)}, f32[24,24]{1,0:T(8,128)S(1)}, f32[1,1]{1,0:T(1,128)}) custom-call(f32[1,24,16,128]{3,2,1,0:T(8,128)S(1)} %copy-done, f32[16,128]{1,0:T(8,128)S(1)} %copy-done.2, f32[16,128]{1,0:T(8,128)S(1)} %copy-done.3, f32[24,24]{1,0:T(8,128)S(1)} %copy-done.1, s32[4,1,8]{2,1,0:T(1,128)S(1)} %copy-done.4), custom_call_target="tpu_custom_call" | custom-call | tf_op jit(solution)/shard_map/pallas_call | solution.py:436
  34.1 0.6 %copy.11 = f32[16,128]{1,0:T(8,128)} copy(f32[16,128]{1,0:T(8,128)S(1)} %get-tuple-element.12) | data formatting | bytes 16384
  34.7 0.6 %copy.12 = f32[24,24]{1,0:T(8,128)} copy(f32[24,24]{1,0:T(8,128)S(1)} %get-tuple-element.13) | data formatting | bytes 4608
Async XLA Ops:
  0.6 0.9 %copy-start = (f32[1,24,16,128]{3,2,1,0:T(8,128)S(1)}, f32[1,24,16,128]{3,2,1,0:T(8,128)}, u32[]{:S(2)}) copy-start(f32[1,24,16,128]{3,2,1,0:T(8,128)} %tracer_ref.1) | copy-start | bytes 589828
  1.6 0.7 %copy-start.1 = (f32[24,24]{1,0:T(8,128)S(1)}, f32[24,24]{1,0:T(8,128)}, u32[]{:S(2)}) copy-start(f32[24,24]{1,0:T(8,128)} %weight_ref.1) | copy-start | bytes 6916
  2.3 0.7 %copy-start.2 = (f32[16,128]{1,0:T(8,128)S(1)}, f32[16,128]{1,0:T(8,128)}, u32[]{:S(2)}) copy-start(f32[16,128]{1,0:T(8,128)} %kappa_ref.1) | copy-start | bytes 24580
  3.0 0.7 %copy-start.3 = (f32[16,128]{1,0:T(8,128)S(1)}, f32[16,128]{1,0:T(8,128)}, u32[]{:S(2)}) copy-start(f32[16,128]{1,0:T(8,128)} %dkappa_ref.1) | copy-start | bytes 24580
  3.7 0.7 %copy-start.4 = (s32[4,1,8]{2,1,0:T(1,128)S(1)}, s32[4,1,8]{2,1,0:T(1,128)}, u32[]{:S(2)}) copy-start(s32[4,1,8]{2,1,0:T(1,128)} %observed_ref.1) | copy-start | bytes 388

commit v2 on v1

--- a/solution.py
+++ b/solution.py
@@ -230,22 +230,7 @@
     energy = dkappa_ref[...] * reg
     energy = energy[0:8] + energy[8:16]
 
-    for copy in copies[:8]:
-        copy.wait_recv()
-
-    for g in range(4):
-        held = jnp.where(lane % 16 < 8, rim[1, g], rim[0, g]) * inside_rim
-        for s in range(8):
-            e = 8 * g + s
-            turn = (112 - 16 * s) % LANES
-            part = held if turn == 0 else pltpu.roll(held, turn, 2)
-            cell = sides(mb[0, e], part)
-            if e < 24:
-                sb[0, e] = cell
-            if e >= 8:
-                sb[0, e - 8] = sb[0, e - 8] + pltpu.roll(cell, 64, 2)
-
-    def forward(rows, base, tan, coef, dom, k):
+    def forward(lo, hi, base, tan, coef, dom, k):
         def body(r, n):
             b = base[k, pl.ds(r - 1, n + 2)]
             mid = b[1:-1]
@@ -273,11 +258,30 @@
                 fe = fe + ke * (east(tmid) - tmid)
                 tan[k, pl.ds(r, n)] = tmid + close(fs, fe)
 
-        sweep(k + 1, rows - k - 1, 4, body)
+        sweep(lo, hi, 4, body)
 
     for k in range(STEPS):
-        forward(32, mb, mt, mc, None, k)
-        forward(24, sb, st, sc, domain, k)
+        forward(9 + k, 23 - k, mb, mt, mc, None, k)
+
+    for copy in copies[:8]:
+        copy.wait_recv()
+
+    for g in range(4):
+        held = jnp.where(lane % 16 < 8, rim[1, g], rim[0, g]) * inside_rim
+        for s in range(8):
+            e = 8 * g + s
+            turn = (112 - 16 * s) % LANES
+            part = held if turn == 0 else pltpu.roll(held, turn, 2)
+            cell = sides(mb[0, e], part)
+            if e < 24:
+                sb[0, e] = cell
+            if e >= 8:
+                sb[0, e - 8] = sb[0, e - 8] + pltpu.roll(cell, 64, 2)
+
+    for k in range(STEPS):
+        forward(k + 1, 9 + k, mb, mt, mc, None, k)
+        forward(23 - k, 31 - k, mb, mt, mc, None, k)
+        forward(k + 1, 23 - k, sb, st, sc, domain, k)
 
     main_cells = jnp.where((lane >= 8) & (lane < 120), 1.0, 0.0).astype(F32)
     side_cells = jnp.where(

time: 37.4 us -> 37.2 us (level)
  no operation moved by 1% of the time
where the time goes in v2:
time: 37.2 us; the launch traced here: 36.8 us
  Pallas kernels  29.6 us (80%)
  local copies, waits for them, and re-layouts  4.9 us (13%)
  between operations  2.34 us (6%)
    pallas_call x1, Pallas kernels, body(): pl.pallas_call(functools.partial(kernel, nx, ny), out_shape=(jax.ShapeDty...  29.6 us
    unnamed x12, local copies, waits for them, and re-layouts  4.9 us

profile of v2, /device:TPU:0, one launch (start us, length us, event | category | flops | bytes accessed | tf_op | source)
XLA Modules:
  0.0 36.8 jit_solution(2976472531135852149)
XLA Ops:
  0.6 0.0 copy-start
  0.6 0.9 %copy-done = f32[1,24,16,128]{3,2,1,0:T(8,128)S(1)} copy-done((f32[1,24,16,128]{3,2,1,0:T(8,128)S(1)}, f32[1,24,16,128]{3,2,1,0:T(8,128)}, u32[]{:S(2)}) %copy-start) | copy-done | bytes 196632
  1.6 0.0 copy-start.1
  1.6 0.7 %copy-done.1 = f32[24,24]{1,0:T(8,128)S(1)} copy-done((f32[24,24]{1,0:T(8,128)S(1)}, f32[24,24]{1,0:T(8,128)}, u32[]{:S(2)}) %copy-start.1) | copy-done | bytes 2328
  2.3 0.0 copy-start.2
  2.3 0.7 %copy-done.2 = f32[16,128]{1,0:T(8,128)S(1)} copy-done((f32[16,128]{1,0:T(8,128)S(1)}, f32[16,128]{1,0:T(8,128)}, u32[]{:S(2)}) %copy-start.2) | copy-done | bytes 8216
  3.0 0.0 copy-start.3
  3.0 0.7 %copy-done.3 = f32[16,128]{1,0:T(8,128)S(1)} copy-done((f32[16,128]{1,0:T(8,128)S(1)}, f32[16,128]{1,0:T(8,128)}, u32[]{:S(2)}) %copy-start.3) | copy-done | bytes 8216
  3.7 0.0 copy-start.4
  3.7 0.7 %copy-done.4 = s32[4,1,8]{2,1,0:T(1,128)S(1)} copy-done((s32[4,1,8]{2,1,0:T(1,128)S(1)}, s32[4,1,8]{2,1,0:T(1,128)}, u32[]{:S(2)}) %copy-start.4) | copy-done | bytes 152
  4.3 29.6 %shard_map.76 = (f32[16,128]{1,0:T(8,128)S(1)}, f32[24,24]{1,0:T(8,128)S(1)}, f32[1,1]{1,0:T(1,128)}) custom-call(f32[1,24,16,128]{3,2,1,0:T(8,128)S(1)} %copy-done, f32[16,128]{1,0:T(8,128)S(1)} %copy-done.2, f32[16,128]{1,0:T(8,128)S(1)} %copy-done.3, f32[24,24]{1,0:T(8,128)S(1)} %copy-done.1, s32[4,1,8]{2,1,0:T(1,128)S(1)} %copy-done.4), custom_call_target="tpu_custom_call" | custom-call | tf_op jit(solution)/shard_map/pallas_call | solution.py:440
  33.9 0.6 %copy.11 = f32[16,128]{1,0:T(8,128)} copy(f32[16,128]{1,0:T(8,128)S(1)} %get-tuple-element.12) | data formatting | bytes 16384
  34.5 0.6 %copy.12 = f32[24,24]{1,0:T(8,128)} copy(f32[24,24]{1,0:T(8,128)S(1)} %get-tuple-element.13) | data formatting | bytes 4608
Async XLA Ops:
  0.6 0.9 %copy-start = (f32[1,24,16,128]{3,2,1,0:T(8,128)S(1)}, f32[1,24,16,128]{3,2,1,0:T(8,128)}, u32[]{:S(2)}) copy-start(f32[1,24,16,128]{3,2,1,0:T(8,128)} %tracer_ref.1) | copy-start | bytes 589828
  1.6 0.7 %copy-start.1 = (f32[24,24]{1,0:T(8,128)S(1)}, f32[24,24]{1,0:T(8,128)}, u32[]{:S(2)}) copy-start(f32[24,24]{1,0:T(8,128)} %weight_ref.1) | copy-start | bytes 6916
  2.3 0.7 %copy-start.2 = (f32[16,128]{1,0:T(8,128)S(1)}, f32[16,128]{1,0:T(8,128)}, u32[]{:S(2)}) copy-start(f32[16,128]{1,0:T(8,128)} %kappa_ref.1) | copy-start | bytes 24580
  3.0 0.7 %copy-start.3 = (f32[16,128]{1,0:T(8,128)S(1)}, f32[16,128]{1,0:T(8,128)}, u32[]{:S(2)}) copy-start(f32[16,128]{1,0:T(8,128)} %dkappa_ref.1) | copy-start | bytes 24580
  3.7 0.7 %copy-start.4 = (s32[4,1,8]{2,1,0:T(1,128)S(1)}, s32[4,1,8]{2,1,0:T(1,128)}, u32[]{:S(2)}) copy-start(s32[4,1,8]{2,1,0:T(1,128)} %observed_ref.1) | copy-start | bytes 388
